TPU v7x, 256 devices: a whole 4x4x8 slice. The times are simulated.
256 devices in a mesh: lat: 32 (over y_lo, z, core), lon: 8 (over x, y_hi).
Axes of the slice: x: 4, y: 4 (y_hi: 2, y_lo: 2; y = y_hi * 2 + y_lo), z: 8, core: 2. Of those that a mesh axis runs over, the one named last changes fastest.
Arguments:
- signal: bfloat16 [768, 64, 1024], P(None, 'lat', 'lon'), may hold values from -6 to 6
- gate_input: bfloat16 [768, 64, 1024], P(None, 'lat', 'lon'), may hold values from -6 to 6
- cotangent: bfloat16 [768, 64, 1024], P(None, 'lat', 'lon'), may hold values from -6 to 6
- zonal_taps: bfloat16 [768, 256], P('lat'), may hold values from -0.375 to 0.375
- meridional_taps: float32 [768, 128], P('lat'), may hold values from -0.75 to 0.75
Outputs:
- mixed: bfloat16 [768, 64, 1024], P(None, 'lat', 'lon')
- gate_grad: bfloat16 [768, 64, 1024], P(None, 'lat', 'lon')
- signal_grad: bfloat16 [768, 64, 1024], P(None, 'lat', 'lon')
- zonal_grad: float32 [768, 256], P('lat')
- meridional_grad: float32 [768, 128], P('lat')
All inputs are finite; a program needn't handle non-finite values.
Results may differ from a plain program's by a relative error of at most 0.015.
Values may be sent and summed in bfloat16 or wider, within the bound.
A program may use at most 64 MiB of HBM per device.

v0:
```python
import math

import jax
import jax.numpy as jnp
from jax import lax
from jax.sharding import PartitionSpec as P

HIGHEST = lax.Precision.HIGHEST


def padded(x, sides, width):
    for axis, dim in sides:
        peers, length = (lax.axis_size(axis), x.shape[dim])
        up = [(i, (i + 1) % peers) for i in range(peers)]
        down = [(j, i) for i, j in up]
        last = lax.slice_in_dim(x, length - width, length, axis=dim)
        leading = lax.slice_in_dim(x, 0, width, axis=dim)
        before = lax.ppermute(last, axis, up)
        after = lax.ppermute(leading, axis, down)
        x = jnp.concatenate([before, x, after], axis=dim)
    return x


def skew_matrix(pattern, row_count, col_count, first_col):
    channels_here, period = pattern.shape
    tiled = jnp.tile(pattern, (1, row_count))
    windows = tiled[:, : row_count * (period - 1)].reshape(channels_here, row_count, period - 1)
    return windows[:, :, first_col : first_col + col_count]


def diagonal_sums(product, tap_count):
    blocks, height, across = product.shape
    flattened = product.reshape(blocks, height * across)
    flattened = jnp.pad(flattened, ((0, 0), (0, height)))
    skewed = flattened.reshape(blocks, height, across + 1)
    return jnp.sum(skewed[:, :, :tap_count], axis=1)


def latitude_bins(cross_terms):
    blocks, latitudes, _ = cross_terms.shape
    widened = jnp.pad(cross_terms, ((0, 0), (0, 0), (0, latitudes)))
    flattened = widened.reshape(blocks, 2 * latitudes * latitudes)
    flattened = jnp.pad(flattened, ((0, 0), (0, latitudes)))
    skewed = flattened.reshape(blocks, latitudes, 2 * latitudes + 1)
    column_sums = jnp.sum(skewed, axis=1)
    reversed_sums = column_sums[:, ::-1]
    return jnp.concatenate(
        [
            column_sums[:, :1],
            reversed_sums[:, :latitudes],
            reversed_sums[:, latitudes + 1 : 2 * latitudes],
        ],
        axis=1,
    )


def on_device(signal, gate_input, cotangent, zonal_taps, meridional_taps):
    pencil_signal, pencil_gate, pencil_cotangent = (
        lax.all_to_all(signal, "lat", split_axis=0, concat_axis=1, tiled=True),
        lax.all_to_all(gate_input, "lat", split_axis=0, concat_axis=1, tiled=True),
        lax.all_to_all(cotangent, "lat", split_axis=0, concat_axis=1, tiled=True),
    )
    conv_grad = (pencil_cotangent.astype(jnp.float32) * pencil_gate.astype(jnp.float32)).astype(
        jnp.bfloat16
    )
    channels_here = zonal_taps.shape[0]
    tap_count = zonal_taps.shape[1]
    reach_cols = tap_count // 2
    latitudes = pencil_signal.shape[1]
    columns = pencil_signal.shape[2]
    extended = padded(pencil_signal, (("lon", 2),), reach_cols)
    zero_block = jnp.zeros((channels_here, columns), zonal_taps.dtype)
    forward_pattern = jnp.concatenate([zero_block, zonal_taps[:, ::-1], zero_block], axis=1)
    forward_block = skew_matrix(forward_pattern, columns, columns + tap_count, columns - 1)
    filtered = jnp.einsum(
        "cjk,cak->caj", forward_block, extended, preferred_element_type=jnp.float32
    )
    wrapped = jnp.concatenate(
        [meridional_taps[:, latitudes + 1 :], meridional_taps[:, :latitudes]], axis=1
    )
    lat_pattern = jnp.concatenate(
        [wrapped[:, ::-1], jnp.zeros((channels_here, 1), jnp.float32)], axis=1
    )
    lat_block = skew_matrix(lat_pattern, latitudes, latitudes, latitudes - 1)
    convolved = jnp.einsum("cnm,cml->cnl", lat_block, filtered, precision=HIGHEST)
    convolved_round = convolved.astype(jnp.bfloat16)
    conv_float = conv_grad.astype(jnp.float32)
    filtered_grad = jnp.einsum("cnm,cnl->cml", lat_block, conv_float, precision=HIGHEST)
    rounded_grad = filtered_grad.astype(jnp.bfloat16)
    cross_terms = jnp.einsum("cnl,cml->cnm", conv_float, filtered, precision=HIGHEST)
    meridional_part = latitude_bins(cross_terms)
    grad_extended = padded(rounded_grad, (("lon", 2),), reach_cols)
    backward_pattern = jnp.concatenate(
        [zero_block[:, 1:], zonal_taps, zero_block, zero_block[:, :1]], axis=1
    )
    backward_block = skew_matrix(backward_pattern, columns, columns + tap_count, columns - 1)
    signal_grad = jnp.einsum(
        "cjk,cak->caj", backward_block, grad_extended, preferred_element_type=jnp.float32
    ).astype(jnp.bfloat16)
    product = jnp.einsum(
        "caj,cak->cjk", pencil_signal, grad_extended, preferred_element_type=jnp.float32
    )
    zonal_part = diagonal_sums(product, tap_count)
    zonal_sum, meridional_sum = (
        lax.psum(zonal_part.astype(jnp.bfloat16), "lon").astype(jnp.float32),
        lax.psum(meridional_part.astype(jnp.bfloat16), "lon").astype(jnp.float32),
    )
    factor = 1.0 / math.sqrt(latitudes * columns * lax.axis_size("lon"))
    convolved_back = convolved_round.astype(jnp.float32)
    mixed = (pencil_gate.astype(jnp.float32) * convolved_back).astype(jnp.bfloat16)
    gate_grad = (pencil_cotangent.astype(jnp.float32) * convolved_back).astype(jnp.bfloat16)
    band_mixed, band_gate_grad, band_signal_grad = (
        lax.all_to_all(mixed, "lat", split_axis=1, concat_axis=0, tiled=True),
        lax.all_to_all(gate_grad, "lat", split_axis=1, concat_axis=0, tiled=True),
        lax.all_to_all(signal_grad, "lat", split_axis=1, concat_axis=0, tiled=True),
    )
    return (
        band_mixed,
        band_gate_grad,
        band_signal_grad,
        zonal_sum * factor,
        meridional_sum * factor,
    )


def solution(mesh):
    return jax.shard_map(
        on_device,
        mesh=mesh,
        in_specs=(
            P(None, "lat", "lon"),
            P(None, "lat", "lon"),
            P(None, "lat", "lon"),
            P("lat", None),
            P("lat", None),
        ),
        out_specs=(
            P(None, "lat", "lon"),
            P(None, "lat", "lon"),
            P(None, "lat", "lon"),
            P("lat", None),
            P("lat", None),
        ),
        check_vma=False,
    )
```

profile of v0, /device:TPU:32, one launch (start us, length us, event | category | flops | bytes accessed | tf_op | source)
XLA Modules:
  0.0 221.6 jit_solution(6197725613942838766)
XLA Ops:
  0.7 24.7 %all_to_all.90 = bf16[768,2,128]{2,1,0:T(2,128)(2,1)S(1)} all-to-all(bf16[768,2,128]{2,1,0:T(2,128)(2,1)} %param.5), channel_id=1, replica_groups=mesh['lat'=32,'lon'=8] {'lat'}, dimensions={0} | all-to-all | bytes 786432 | tf_op jit(solution)/shard_map/all_to_all | solution.py:59
  25.4 20.5 %all_to_all.91 = bf16[768,2,128]{2,1,0:T(2,128)(2,1)} all-to-all(bf16[768,2,128]{2,1,0:T(2,128)(2,1)} %param.7), channel_id=1, replica_groups=mesh['lat'=32,'lon'=8] {'lat'}, dimensions={0} | all-to-all | bytes 786432 | tf_op jit(solution)/shard_map/all_to_all | solution.py:61
  45.8 5.4 %all-to-all-start = ((bf16[768,2,128]{2,1,0:T(2,128)(2,1)}), bf16[768,2,128]{2,1,0:T(2,128)(2,1)}, u32[]{:S(2)}, u32[]{:S(2)}) async-start(bf16[768,2,128]{2,1,0:T(2,128)(2,1)} %param.6), calls=%async_computation | async-start | bytes 786432 | tf_op jit(solution)/shard_map/all_to_all | solution.py:60
  51.6 5.2 %collective-permute-start.1 = (bf16[24,64,128]{2,1,0:T(8,128)(2,1)S(1)}, bf16[24,64,128]{2,1,0:T(8,128)(2,1)}, u32[]{:S(2)}, u32[]{:S(2)}) collective-permute-start(bf16[24,64,128]{2,1,0:T(8,128)(2,1)S(1)} %bitcast.63), channel_id=1, source_target_pairs={{1,0},{2,1},{3,2},{4,3},{5,4},{6,5},{7,6},{0,7},{9,8},{10,9},{11,1... | collective-permute-start | bytes 1179656 | tf_op jit(solution)/shard_map/ppermute | solution.py:19
  57.8 2.4 %reshape.51 = f32[24,64,127]{2,1,0:T(8,128)} reshape(f32[24,8128]{1,0:T(8,128)S(1)} %bitcast.58) | data formatting | bytes 1560576 | tf_op jit(solution)/shard_map/reshape | solution.py:27
  61.2 1.8 copy.38
  63.1 6.9 %reshape.52 = bf16[24,128,511]{2,1,0:T(8,128)(2,1)} reshape(bf16[24,65408]{1,0:T(8,128)(2,1)S(1)} %slice.63) | data formatting | bytes 6279168 | tf_op jit(solution)/shard_map/reshape | solution.py:27
  70.1 1.4 copy.29
  71.5 1.4 copy.25
  72.9 3.7 %collective-permute-done.1 = bf16[24,64,128]{2,1,0:T(8,128)(2,1)} collective-permute-done((bf16[24,64,128]{2,1,0:T(8,128)(2,1)S(1)}, bf16[24,64,128]{2,1,0:T(8,128)(2,1)}, u32[]{:S(2)}, u32[]{:S(2)}) %collective-permute-start.1) | collective-permute-done | bytes 393248 | tf_op jit(solution)/shard_map/ppermute | solution.py:19
  76.6 3.3 %fusion.2 = f32[24,64,128]{2,1,0:T(8,128)S(1)} fusion(bf16[24,128,511]{2,1,0:T(8,128)(2,1)} %reshape.52, bf16[24,64,128]{2,1,0:T(8,128)(2,1)} %collective-permute-done.1, bf16[24,64,128]{2,1,0:T(8,128)(2,1)S(1)} %bitcast.65, bf16[24,64,128]{2,1,0:T(8,128)(2,1)} %collective-permute-done), kind=kOutput, calls=%fused_computation.3 | convolution fusion | flops 154533888 | bytes 4325376 | tf_op jit(solution)/shard_map/cjk,cak->caj/dot_general | solution.py:75
  79.9 1.1 multiply_convert_fusion
  82.1 7.9 %all-to-all-start.2 = ((bf16[24,64,128]{2,0,1:T(8,128)(2,1)}), bf16[24,64,128]{2,0,1:T(8,128)(2,1)S(1)}, u32[]{:S(2)}, u32[]{:S(2)}) async-start(bf16[24,64,128]{2,0,1:T(8,128)(2,1)} %copy.27), calls=%async_computation.2 | async-start | bytes 786432 | tf_op jit(solution)/shard_map/all_to_all | solution.py:113
  91.0 13.9 %all-to-all-done.2 = bf16[24,64,128]{2,0,1:T(8,128)(2,1)S(1)} async-done(((bf16[24,64,128]{2,0,1:T(8,128)(2,1)}), bf16[24,64,128]{2,0,1:T(8,128)(2,1)S(1)}, u32[]{:S(2)}, u32[]{:S(2)}) %all-to-all-start.2) | async-done | bytes 393248 | tf_op jit(solution)/shard_map/all_to_all | solution.py:113
  105.0 5.4 %all-to-all-start.4 = ((bf16[24,64,128]{2,0,1:T(8,128)(2,1)}), bf16[24,64,128]{2,0,1:T(8,128)(2,1)}, u32[]{:S(2)}, u32[]{:S(2)}) async-start(bf16[24,64,128]{2,0,1:T(8,128)(2,1)} %copy.30), calls=%async_computation.4 | async-start | bytes 786432 | tf_op jit(solution)/shard_map/all_to_all | solution.py:114
  110.3 1.8 convolution_convert_fusion
  112.1 4.8 %collective-permute-start.3 = (bf16[24,64,128]{2,1,0:T(8,128)(2,1)}, bf16[24,64,128]{2,1,0:T(8,128)(2,1)}, u32[]{:S(2)}, u32[]{:S(2)}) collective-permute-start(bf16[24,64,128]{2,1,0:T(8,128)(2,1)} %convolution_convert_fusion), channel_id=1, source_target_pairs={{1,0},{2,1},{3,2},{4,3},{5,4},{6,5},{7,6},{0,7},{9,8},{10,9},{11,1... | collective-permute-start | bytes 1179656 | tf_op jit(solution)/shard_map/ppermute | solution.py:19
  117.2 1.8 copy.39
  119.2 6.9 %reshape.53 = bf16[24,128,511]{2,1,0:T(8,128)(2,1)} reshape(bf16[24,65408]{1,0:T(8,128)(2,1)S(1)} %slice.65) | data formatting | bytes 6279168 | tf_op jit(solution)/shard_map/reshape | solution.py:27
  126.1 1.9 fusion.18
  128.6 2.0 reshape.57
  131.2 5.4 %collective-permute-done.3 = bf16[24,64,128]{2,1,0:T(8,128)(2,1)} collective-permute-done((bf16[24,64,128]{2,1,0:T(8,128)(2,1)}, bf16[24,64,128]{2,1,0:T(8,128)(2,1)}, u32[]{:S(2)}, u32[]{:S(2)}) %collective-permute-start.3) | collective-permute-done | bytes 393248 | tf_op jit(solution)/shard_map/ppermute | solution.py:19
  136.6 3.4 %fusion.4 = bf16[24,64,128]{2,1,0:T(8,128)(2,1)S(1)} fusion(bf16[24,128,511]{2,1,0:T(8,128)(2,1)} %reshape.53, bf16[24,64,128]{2,1,0:T(8,128)(2,1)} %collective-permute-done.3, bf16[24,64,128]{2,1,0:T(8,128)(2,1)} %convolution_convert_fusion, bf16[24,64,128]{2,1,0:T(8,128)(2,1)} %collective-permute-done.2), kind=kOutput, calls=%fused_computation.6 | convolution fusion | flops 154730496 | bytes 3932160 | tf_op jit(solution)/shard_map/cjk,cak->caj/dot_general | solution.py:97
  141.1 7.6 %all-to-all-start.5 = ((bf16[24,64,128]{2,0,1:T(8,128)(2,1)}), bf16[24,64,128]{2,0,1:T(8,128)(2,1)S(1)}, u32[]{:S(2)}, u32[]{:S(2)}) async-start(bf16[24,64,128]{2,0,1:T(8,128)(2,1)} %copy.33), calls=%async_computation.5 | async-start | bytes 786432 | tf_op jit(solution)/shard_map/all_to_all | solution.py:115
  148.7 4.2 %convolution_bitcast_fusion = f32[24,128,384]{1,2,0:T(8,128)} fusion(bf16[24,64,128]{2,1,0:T(8,128)(2,1)S(1)} %bitcast.66, bf16[24,64,128]{2,1,0:T(8,128)(2,1)} %collective-permute-done.3, bf16[24,64,128]{2,1,0:T(8,128)(2,1)} %convolution_convert_fusion, bf16[24,64,128]{2,1,0:T(8,128)(2,1)} %collective-permute-done.2), kind=kOutput, calls=%fused_computation.5 | convolution fusion | flops 154533888 | bytes 6291456 | tf_op jit(solution)/shard_map/caj,cak->cjk/dot_general | solution.py:100
  152.9 6.1 %copy.40 = f32[3,8,128,384]{3,1,2,0:T(8,128)} copy(f32[3,8,128,384]{2,3,1,0:T(8,128)} %bitcast.52) | data formatting | bytes 9437184
  159.0 4.8 %pad.13 = f32[24,49280]{1,0:T(8,128)} pad(f32[24,49152]{1,0:T(8,128)} %bitcast.51, f32[]{:T(128)} %constant.3.clone.1), padding=0_0x0_128 | pad | bytes 9449476 | tf_op jit(solution)/shard_map/jit(_pad)/pad | solution.py:34
  163.8 8.1 %reshape.55 = f32[24,128,385]{2,1,0:T(8,128)} reshape(f32[24,49280]{1,0:T(8,128)} %pad.13) | data formatting | bytes 9461760 | tf_op jit(solution)/shard_map/reshape | solution.py:35
  172.0 2.2 slice_reduce_fusion
  174.2 42.1 %all-reduce.4 = (bf16[24,256]{1,0:T(8,128)(2,1)S(1)}, bf16[24,128]{1,0:T(8,128)(2,1)S(1)}) all-reduce(bf16[24,256]{1,0:T(8,128)(2,1)S(1)} %slice_reduce_fusion, bf16[24,128]{1,0:T(8,128)(2,1)S(1)} %pad_maximum_fusion.5), channel_id=1, replica_groups=mesh['lat'=32,'lon'=8] {'lon'}, use_global_device_ids=true, to_apply=%region_1.2 | all-reduce | flops 9216 | bytes 36864 | tf_op jit(solution)/shard_map/psum | solution.py:105
  218.5 2.0 copy.31
  220.6 1.0 copy.34
  (58 shorter events, 9.5 us)
Async XLA Ops:
  0.6 56.2 %copy-start.7 = (bf16[24,256]{1,0:T(8,128)(2,1)S(1)}, bf16[24,256]{1,0:T(8,128)(2,1)}, u32[]{:S(2)}) copy-start(bf16[24,256]{1,0:T(8,128)(2,1)} %param.8) | copy-start | bytes 36868
  0.6 56.4 %copy-start.8 = (f32[24,128]{1,0:T(8,128)S(1)}, f32[24,128]{1,0:T(8,128)}, u32[]{:S(2)}) copy-start(f32[24,128]{1,0:T(8,128)} %param.9) | copy-start | bytes 36868
  45.8 25.7 %all-to-all-start = ((bf16[768,2,128]{2,1,0:T(2,128)(2,1)}), bf16[768,2,128]{2,1,0:T(2,128)(2,1)}, u32[]{:S(2)}, u32[]{:S(2)}) async-start(bf16[768,2,128]{2,1,0:T(2,128)(2,1)} %param.6), calls=%async_computation | async-start | bytes 786432 | tf_op jit(solution)/shard_map/all_to_all | solution.py:60
  51.6 25.0 %copy-start.2 = (bf16[32,24,2,128]{3,2,0,1:T(2,128)(2,1)}, bf16[32,24,2,128]{3,2,0,1:T(2,128)(2,1)S(1)}, u32[]{:S(2)}) copy-start(bf16[32,24,2,128]{3,2,0,1:T(2,128)(2,1)S(1)} %copy.26) | copy-start | bytes 1179652
  51.6 25.0 %collective-permute-start.1 = (bf16[24,64,128]{2,1,0:T(8,128)(2,1)S(1)}, bf16[24,64,128]{2,1,0:T(8,128)(2,1)}, u32[]{:S(2)}, u32[]{:S(2)}) collective-permute-start(bf16[24,64,128]{2,1,0:T(8,128)(2,1)S(1)} %bitcast.63), channel_id=1, source_target_pairs={{1,0},{2,1},{3,2},{4,3},{5,4},{6,5},{7,6},{0,7},{9,8},{10,9},{11,1... | collective-permute-start | bytes 1179656 | tf_op jit(solution)/shard_map/ppermute | solution.py:19
  56.8 19.8 %collective-permute-start = (bf16[24,64,128]{2,1,0:T(8,128)(2,1)S(1)}, bf16[24,64,128]{2,1,0:T(8,128)(2,1)}, u32[]{:S(2)}, u32[]{:S(2)}) collective-permute-start(bf16[24,64,128]{2,1,0:T(8,128)(2,1)S(1)} %bitcast.64), channel_id=1, source_target_pairs={{0,1},{1,2},{2,3},{3,4},{4,5},{5,6},{6,7},{7,0},{8,9},{9,10},{10,1... | collective-permute-start | bytes 1179656 | tf_op jit(solution)/shard_map/ppermute | solution.py:18
  72.9 7.0 %copy-start = (f32[24,64,127]{2,1,0:T(8,128)S(1)}, f32[24,64,127]{2,1,0:T(8,128)}, u32[]{:S(2)}) copy-start(f32[24,64,127]{2,1,0:T(8,128)} %reshape.51) | copy-start | bytes 2340868
  79.9 1.1 copy-start.1
  81.1 35.9 %copy-start.6 = (bf16[24,512]{1,0:T(8,128)(2,1)S(1)}, bf16[24,512]{1,0:T(8,128)(2,1)}, u32[]{:S(2)}) copy-start(bf16[24,512]{1,0:T(8,128)(2,1)} %get-tuple-element.10) | copy-start | bytes 73732
  82.1 22.9 %all-to-all-start.2 = ((bf16[24,64,128]{2,0,1:T(8,128)(2,1)}), bf16[24,64,128]{2,0,1:T(8,128)(2,1)S(1)}, u32[]{:S(2)}, u32[]{:S(2)}) async-start(bf16[24,64,128]{2,0,1:T(8,128)(2,1)} %copy.27), calls=%async_computation.2 | async-start | bytes 786432 | tf_op jit(solution)/shard_map/all_to_all | solution.py:113
  105.0 12.3 %copy-start.4 = (bf16[24,64,128]{2,0,1:T(8,128)(2,1)}, bf16[24,64,128]{2,0,1:T(8,128)(2,1)S(1)}, u32[]{:S(2)}) copy-start(bf16[24,64,128]{2,0,1:T(8,128)(2,1)S(1)} %all-to-all-done.2) | copy-start | bytes 1179652
  105.0 36.1 %all-to-all-start.4 = ((bf16[24,64,128]{2,0,1:T(8,128)(2,1)}), bf16[24,64,128]{2,0,1:T(8,128)(2,1)}, u32[]{:S(2)}, u32[]{:S(2)}) async-start(bf16[24,64,128]{2,0,1:T(8,128)(2,1)} %copy.30), calls=%async_computation.4 | async-start | bytes 786432 | tf_op jit(solution)/shard_map/all_to_all | solution.py:114
  112.1 24.5 %collective-permute-start.3 = (bf16[24,64,128]{2,1,0:T(8,128)(2,1)}, bf16[24,64,128]{2,1,0:T(8,128)(2,1)}, u32[]{:S(2)}, u32[]{:S(2)}) collective-permute-start(bf16[24,64,128]{2,1,0:T(8,128)(2,1)} %convolution_convert_fusion), channel_id=1, source_target_pairs={{1,0},{2,1},{3,2},{4,3},{5,4},{6,5},{7,6},{0,7},{9,8},{10,9},{11,1... | collective-permute-start | bytes 1179656 | tf_op jit(solution)/shard_map/ppermute | solution.py:19
  117.0 19.6 %collective-permute-start.2 = (bf16[24,64,128]{2,1,0:T(8,128)(2,1)}, bf16[24,64,128]{2,1,0:T(8,128)(2,1)}, u32[]{:S(2)}, u32[]{:S(2)}) collective-permute-start(bf16[24,64,128]{2,1,0:T(8,128)(2,1)} %convolution_convert_fusion), channel_id=1, source_target_pairs={{0,1},{1,2},{2,3},{3,4},{4,5},{5,6},{6,7},{7,0},{8,9},{9,10},{10,1... | collective-permute-start | bytes 1179656 | tf_op jit(solution)/shard_map/ppermute | solution.py:18
  131.2 17.4 %copy-start.3 = (bf16[32,24,2,128]{3,2,0,1:T(2,128)(2,1)S(1)}, bf16[32,24,2,128]{3,2,0,1:T(2,128)(2,1)}, u32[]{:S(2)}) copy-start(bf16[32,24,2,128]{3,2,0,1:T(2,128)(2,1)} %copy-done.2) | copy-start | bytes 1179652
  141.1 79.5 %all-to-all-start.5 = ((bf16[24,64,128]{2,0,1:T(8,128)(2,1)}), bf16[24,64,128]{2,0,1:T(8,128)(2,1)S(1)}, u32[]{:S(2)}, u32[]{:S(2)}) async-start(bf16[24,64,128]{2,0,1:T(8,128)(2,1)} %copy.33), calls=%async_computation.5 | async-start | bytes 786432 | tf_op jit(solution)/shard_map/all_to_all | solution.py:115
  172.0 45.5 %copy-start.5 = (bf16[24,64,128]{2,0,1:T(8,128)(2,1)S(1)}, bf16[24,64,128]{2,0,1:T(8,128)(2,1)}, u32[]{:S(2)}) copy-start(bf16[24,64,128]{2,0,1:T(8,128)(2,1)} %copy-done.4) | copy-start | bytes 1179652
where the time goes:
time: 223 us; the launch traced here: 222 us
  blocking collectives  87.3 us (39%)
  local copies, waits for them, and re-layouts  54 us (24%)
  starting transfers between devices  36.3 us (16%)
  waiting for transfers between devices  23 us (10%)
  matrix products  15.7 us (7%)
  other arithmetic  4.42 us (2%)
    psum x1, blocking collectives, on_device(): lax.psum(zonal_part.astype(jnp.bfloat16), 'lon').astype(jnp.float32)  42.1 us
    all_to_all x1, blocking collectives, on_device(): lax.all_to_all(signal, 'lat', split_axis=0, concat_axis=1, tiled=True)  24.7 us
    all_to_all x1, blocking collectives, on_device(): lax.all_to_all(cotangent, 'lat', split_axis=0, concat_axis=1, tiled=True)  20.5 us
    reshape x3, local copies, waits for them, and re-layouts, skew_matrix(): tiled[:, :row_count * (period - 1)]  16.3 us
    all_to_all x1, waiting for transfers between devices, on_device(): lax.all_to_all(mixed, 'lat', split_axis=1, concat_axis=0, tiled=True)  13.9 us
    unnamed x23, local copies, waits for them, and re-layouts  10.6 us
    ppermute x2, starting transfers between devices, padded(): after = lax.ppermute(leading, axis, down)  10 us
    ppermute x2, waiting for transfers between devices, padded(): after = lax.ppermute(leading, axis, down)  9.05 us
  transfers between devices with their start and end apart: 8, of which 3 were waited for; matrix products, arithmetic and copies ran while one was open for 31% of the time, Pallas kernels for 0%

commit v1 on v0

v1 whole, which is shorter than its diff:
```python
import jax
import jax.numpy as jnp
from jax import lax
from jax.experimental import pallas as pl
from jax.experimental.pallas import tpu as pltpu
from jax.sharding import PartitionSpec as P

MESH = pl.DeviceIdType.MESH
BF16 = jnp.bfloat16
F32 = jnp.float32
LATS, LONS = 32, 8
CHANNELS = 768
GROUP = 24
OWN = 3
ROWS = 64
COLS = 128
Z_STEPS = (1, 7, 2, 6, 3, 5, 4, 0)


def dot(a, b, a_dim=1, b_dim=0):
    return lax.dot_general(
        a, b, (((a_dim,), (b_dim,)), ((), ())), preferred_element_type=F32
    )


def place():
    lat, lon = lax.axis_index("lat"), lax.axis_index("lon")
    return lat, lon


def each_peer(lat, lon, visit):
    y_lo, z, core = lat // 16, (lat // 2) % 8, lat % 2
    x, y = lon // 2, (lon % 2) * 2 + y_lo

    def around(i, carry):
        x_peer, y_peer = (x + i % 4) % 4, (y + (i // 4) % 4) % 4
        lat_base = (y_peer % 2) * 16 + (core + i // 16) % 2
        lon_peer = x_peer * 2 + y_peer // 2
        for step in Z_STEPS:
            lat_peer = lat_base + ((z + step) % 8) * 2
            if step:
                visit(lat_peer, lon_peer)
            else:

                @pl.when(i != 0)
                def _():
                    visit(lat_peer, lon_peer)

        return carry

    lax.fori_loop(0, 32, around, 0)


def reversal(size):
    rows = lax.broadcasted_iota(jnp.int32, (size, size), 0)
    cols = lax.broadcasted_iota(jnp.int32, (size, size), 1)
    return jnp.where(rows + cols == size - 1, 1.0, 0.0).astype(BF16)


def around_circle(blocks):
    return jnp.concatenate(
        [
            jnp.concatenate([blocks[(b + d - 1) % LONS] for d in range(3)], axis=1)
            for b in range(LONS)
        ],
        axis=0,
    )


def mixer(
    signal,
    gate,
    cotangent,
    zonal,
    meridional,
    conv_out,
    grad_out,
    zonal_out,
    meridional_out,
    zonal_rows,
    grad_src,
    signal_in,
    grad_in,
    conv_src,
    result_src,
    ahead,
    back,
    lat_weights,
    taps_src,
    taps_in,
    send,
    recv,
):
    lat, lon = place()
    mine = lat * GROUP + lon * OWN
    barrier = pltpu.get_barrier_semaphore()

    def greet(lat_peer, lon_peer):
        pl.semaphore_signal(
            barrier, inc=1, device_id=(lat_peer, lon_peer), device_id_type=MESH
        )

    each_peer(lat, lon, greet)

    flat = (CHANNELS * 2, COLS)
    product = gate.reshape(*flat)[...].astype(F32) * cotangent.reshape(*flat)[...].astype(F32)
    grad_src.reshape(*flat)[...] = product.astype(BF16)

    pl.semaphore_wait(barrier, LATS * LONS - 1)

    def spread(source, landing, k):
        def to(lat_peer, lon_peer):
            pltpu.make_async_remote_copy(
                source.at[pl.ds(lat_peer * GROUP + lon_peer * OWN, OWN)],
                landing.at[lon, :, lat],
                send.at[k],
                recv.at[k],
                device_id=(lat_peer, lon_peer),
                device_id_type=MESH,
            ).start()

        each_peer(lat, lon, to)
        landing[lon, :, lat] = source[pl.ds(mine, OWN)]

    def give_back(source, landing, k):
        def to(lat_peer, lon_peer):
            pltpu.make_async_remote_copy(
                source.at[lon_peer, :, lat_peer],
                landing.at[pl.ds(mine, OWN)],
                send.at[k],
                recv.at[k],
                device_id=(lat_peer, lon_peer),
                device_id_type=MESH,
            ).start()

        each_peer(lat, lon, to)
        landing[pl.ds(mine, OWN)] = source[lon, :, lat]

    others = signal.at[pl.ds(0, CHANNELS - OWN)]

    def wait_for(semaphore):
        pltpu.make_async_copy(others, others, semaphore).wait()

    spread(signal, signal_in, 0)
    spread(grad_src, grad_in, 1)

    zonal_rows[...] = zonal[...].astype(F32)
    for j in range(OWN):
        row = jnp.concatenate(
            [zonal_rows[pl.ds(lon * OWN + j, 1), :], jnp.zeros((1, 256), F32)], axis=1
        )
        skew = pltpu.roll(
            jnp.broadcast_to(row, (COLS, 512)), 0, 1, stride=1, stride_axis=0
        )
        for d in range(3):
            block = skew[:, 256 - 128 * d : 384 - 128 * d]
            ahead[j, d * COLS : (d + 1) * COLS, :] = block.astype(BF16)
            back[j, (2 - d) * COLS : (3 - d) * COLS, :] = block.T.astype(BF16)
        line = meridional[pl.ds(lon * OWN + j, 1), :]
        turned = pltpu.roll(
            jnp.broadcast_to(line, (ROWS, COLS)), 0, 1, stride=1, stride_axis=0
        )
        lat_weights[j] = turned.astype(BF16)
    flip_cols, flip_rows = reversal(COLS), reversal(ROWS)

    signal_view = signal_in.reshape(LONS, OWN, ROWS, COLS)
    grad_view = grad_in.reshape(LONS, OWN, ROWS, COLS)
    conv_view = conv_src.reshape(LONS, OWN, ROWS, COLS)
    result_view = result_src.reshape(LONS, OWN, ROWS, COLS)

    wait_for(recv.at[0])
    backwards, flipped = [], []
    for j in range(OWN):
        blocks = [signal_view[b, j] for b in range(LONS)]
        filtered = dot(around_circle(blocks), ahead[j]).astype(BF16)
        wide = jnp.concatenate(
            [filtered[b * ROWS : (b + 1) * ROWS] for b in range(LONS)], axis=1
        )
        convolved = dot(lat_weights[j][:, :ROWS], wide, 0, 0).astype(BF16)
        for b in range(LONS):
            conv_view[b, j] = convolved[:, b * COLS : (b + 1) * COLS]
        flipped.append(dot(flip_rows, wide).astype(BF16))
    give_back(conv_src, conv_out, 2)
    for j in range(OWN):
        stack = jnp.concatenate([signal_view[b, j] for b in range(LONS)], axis=0)
        turned = dot(stack, flip_cols).astype(BF16)
        backwards.append([turned[b * ROWS : (b + 1) * ROWS] for b in range(LONS)])

    wait_for(recv.at[1])
    rounded = []
    for j in range(OWN):
        wide = jnp.concatenate([grad_view[b, j] for b in range(LONS)], axis=1)
        gradient = dot(lat_weights[j][:, :ROWS], wide).astype(BF16)
        blocks = [gradient[:, b * COLS : (b + 1) * COLS] for b in range(LONS)]
        rounded.append(jnp.concatenate(blocks, axis=0))
        result = dot(around_circle(blocks), back[j]).astype(BF16)
        for b in range(LONS):
            result_view[b, j] = result[b * ROWS : (b + 1) * ROWS]
    give_back(result_src, grad_out, 3)

    scale = 1.0 / 256.0
    for j in range(OWN):
        products = dot(around_circle(backwards[j]), rounded[j], 0, 0)
        side = jnp.concatenate(
            [products[2 * COLS :], products[COLS : 2 * COLS], products[:COLS], jnp.zeros((COLS, COLS), F32)],
            axis=1,
        )
        diagonals = pltpu.roll(side, 385, 1, stride=1, stride_axis=0)
        taps_src[pl.ds(j, 1), :256] = (
            jnp.sum(diagonals[:, :256], axis=0, keepdims=True) * scale
        )
        wide = jnp.concatenate([grad_view[b, j] for b in range(LONS)], axis=1)
        crossed = dot(flipped[j], wide, 1, 1)
        crossed = jnp.concatenate([crossed, jnp.zeros((ROWS, ROWS), F32)], axis=1)
        diagonals = pltpu.roll(crossed, 65, 1, stride=1, stride_axis=0)
        taps_src[pl.ds(j, 1), 256:] = jnp.sum(diagonals, axis=0, keepdims=True) * scale
    for step in range(1, LONS):
        pltpu.make_async_remote_copy(
            taps_src,
            taps_in.at[lon],
            send.at[4],
            recv.at[4],
            device_id=(lat, (lon + step) % LONS),
            device_id_type=MESH,
        ).start()
    taps_in[lon] = taps_src[...]

    seven = taps_in.at[pl.ds(0, LONS - 1)]
    pltpu.make_async_copy(seven, seven, recv.at[4]).wait()
    for b in range(LONS):
        for j in range(OWN):
            zonal_out[b * OWN + j : b * OWN + j + 1, :] = taps_in[b, j : j + 1, :256]
            meridional_out[b * OWN + j : b * OWN + j + 1, :] = taps_in[b, j : j + 1, 256:]

    wait_for(recv.at[2])
    wait_for(recv.at[3])
    for k in range(4):
        wait_for(send.at[k])
    pltpu.make_async_copy(seven, seven, send.at[4]).wait()


def on_device(signal, gate, cotangent, zonal, meridional):
    field = (CHANNELS, 2, COLS)
    pencil = (LONS, OWN, LATS, 2, COLS)
    in_vmem = pl.BlockSpec(memory_space=pltpu.VMEM)
    convolved, signal_grad, zonal_grad, meridional_grad = pl.pallas_call(
        mixer,
        out_shape=[
            jax.ShapeDtypeStruct(field, BF16),
            jax.ShapeDtypeStruct(field, BF16),
            jax.ShapeDtypeStruct((GROUP, 256), F32),
            jax.ShapeDtypeStruct((GROUP, 128), F32),
        ],
        in_specs=[in_vmem] * 5,
        out_specs=[in_vmem] * 4,
        scratch_shapes=[
            pltpu.VMEM((GROUP, 256), F32),
            pltpu.VMEM(field, BF16),
            pltpu.VMEM(pencil, BF16),
            pltpu.VMEM(pencil, BF16),
            pltpu.VMEM(pencil, BF16),
            pltpu.VMEM(pencil, BF16),
            pltpu.VMEM((OWN, 3 * COLS, COLS), BF16),
            pltpu.VMEM((OWN, 3 * COLS, COLS), BF16),
            pltpu.VMEM((OWN, ROWS, COLS), BF16),
            pltpu.VMEM((8, 384), F32),
            pltpu.VMEM((LONS, 8, 384), F32),
            pltpu.SemaphoreType.DMA((5,)),
            pltpu.SemaphoreType.DMA((5,)),
        ],
        compiler_params=pltpu.CompilerParams(
            collective_id=0, has_side_effects=True, vmem_limit_bytes=32 * 1024 * 1024
        ),
        name="mixer",
    )(signal, gate, cotangent, zonal, meridional)
    wide = convolved.astype(F32)
    mixed = (gate.astype(F32) * wide).astype(BF16)
    gate_grad = (cotangent.astype(F32) * wide).astype(BF16)
    return mixed, gate_grad, signal_grad, zonal_grad, meridional_grad


def solution(mesh):
    fields = P(None, "lat", "lon")
    filters = P("lat", None)
    return jax.shard_map(
        on_device,
        mesh=mesh,
        in_specs=(fields, fields, fields, filters, filters),
        out_specs=(fields, fields, fields, filters, filters),
        check_vma=False,
    )
```

time: 223 us -> 62.9 us (0.28)
  the two profiles are of different devices: /device:TPU:32 before, /device:TPU:1 now
where the time goes in v1:
time: 62.9 us; the launch traced here: 62.6 us
  Pallas kernels  54 us (86%)
  local copies, waits for them, and re-layouts  6.34 us (10%)
  other arithmetic  1.59 us (3%)
  between operations  0.65 us (1%)
    pallas_call x1, Pallas kernels, on_device(): pl.pallas_call(mixer, out_shape=[jax.ShapeDtypeStruct(field, BF16), jax.S...  54 us
    unnamed x13, local copies, waits for them, and re-layouts  6.34 us
    convert_element_type x1, other arithmetic, on_device(): gate_grad = (cotangent.astype(F32) * wide).astype(BF16)  1.59 us

profile of v1, /device:TPU:1, one launch (start us, length us, event | category | flops | bytes accessed | tf_op | source)
XLA Modules:
  0.0 62.6 jit_solution(2859568179444323580)
XLA Ops:
  0.6 0.0 copy-start
  0.6 1.0 %copy-done = bf16[768,2,128]{2,1,0:T(2,128)(2,1)S(1)} copy-done((bf16[768,2,128]{2,1,0:T(2,128)(2,1)S(1)}, bf16[768,2,128]{2,1,0:T(2,128)(2,1)}, u32[]{:S(2)}) %copy-start) | copy-done | bytes 393240
  1.6 0.0 copy-start.1
  1.6 1.0 %copy-done.1 = bf16[768,2,128]{2,1,0:T(2,128)(2,1)S(1)} copy-done((bf16[768,2,128]{2,1,0:T(2,128)(2,1)S(1)}, bf16[768,2,128]{2,1,0:T(2,128)(2,1)}, u32[]{:S(2)}) %copy-start.1) | copy-done | bytes 393240
  2.6 0.0 copy-start.2
  2.6 1.0 %copy-done.2 = bf16[768,2,128]{2,1,0:T(2,128)(2,1)S(1)} copy-done((bf16[768,2,128]{2,1,0:T(2,128)(2,1)S(1)}, bf16[768,2,128]{2,1,0:T(2,128)(2,1)}, u32[]{:S(2)}) %copy-start.2) | copy-done | bytes 393240
  3.6 0.0 copy-start.3
  3.6 0.7 %copy-done.3 = bf16[24,256]{1,0:T(8,128)(2,1)S(1)} copy-done((bf16[24,256]{1,0:T(8,128)(2,1)S(1)}, bf16[24,256]{1,0:T(8,128)(2,1)}, u32[]{:S(2)}) %copy-start.3) | copy-done | bytes 12312
  4.3 0.0 copy-start.4
  4.3 0.7 %copy-done.4 = f32[24,128]{1,0:T(8,128)S(1)} copy-done((f32[24,128]{1,0:T(8,128)S(1)}, f32[24,128]{1,0:T(8,128)}, u32[]{:S(2)}) %copy-start.4) | copy-done | bytes 12312
  5.0 54.0 %mixer.1 = (bf16[768,2,128]{2,1,0:T(2,128)(2,1)S(1)}, bf16[768,2,128]{2,1,0:T(2,128)(2,1)S(1)}, f32[24,256]{1,0:T(8,128)S(1)}, f32[24,128]{1,0:T(8,128)S(1)}) custom-call(bf16[768,2,128]{2,1,0:T(2,128)(2,1)S(1)} %copy-done.2, bf16[768,2,128]{2,1,0:T(2,128)(2,1)S(1)} %copy-done, bf16[768,2,128]{2,1,0:T(2,128)(2,1)S(1)} %copy-done.1, ...), custom_call_target="tpu_custom_call" | custom-call | tf_op jit(solution)/shard_map/mixer/pallas_call | solution.py:246
  59.1 1.6 %fusion.1 = (bf16[768,2,128]{2,1,0:T(2,128)(2,1)}, bf16[768,2,128]{2,1,0:T(2,128)(2,1)}) fusion(bf16[768,2,128]{2,1,0:T(2,128)(2,1)S(1)} %get-tuple-element.9, bf16[768,2,128]{2,1,0:T(2,128)(2,1)S(1)} %copy-done.1, bf16[768,2,128]{2,1,0:T(2,128)(2,1)S(1)} %copy-done), kind=kLoop, calls=%fused_computation.3 | loop fusion | flops 1376256 | bytes 1966080 | tf_op jit(solution)/shard_map/convert_element_type | solution.py:278
  60.7 0.7 %copy.13 = bf16[768,2,128]{2,1,0:T(2,128)(2,1)} copy(bf16[768,2,128]{2,1,0:T(2,128)(2,1)S(1)} %get-tuple-element.22) | data formatting | bytes 786432
  61.4 0.6 copy.14
  62.0 0.6 copy.15
Async XLA Ops:
  0.6 1.0 %copy-start = (bf16[768,2,128]{2,1,0:T(2,128)(2,1)S(1)}, bf16[768,2,128]{2,1,0:T(2,128)(2,1)}, u32[]{:S(2)}) copy-start(bf16[768,2,128]{2,1,0:T(2,128)(2,1)} %gate.1) | copy-start | bytes 1179652
  1.6 1.0 %copy-start.1 = (bf16[768,2,128]{2,1,0:T(2,128)(2,1)S(1)}, bf16[768,2,128]{2,1,0:T(2,128)(2,1)}, u32[]{:S(2)}) copy-start(bf16[768,2,128]{2,1,0:T(2,128)(2,1)} %cotangent.1) | copy-start | bytes 1179652
  2.6 1.0 %copy-start.2 = (bf16[768,2,128]{2,1,0:T(2,128)(2,1)S(1)}, bf16[768,2,128]{2,1,0:T(2,128)(2,1)}, u32[]{:S(2)}) copy-start(bf16[768,2,128]{2,1,0:T(2,128)(2,1)} %signal.1) | copy-start | bytes 1179652
  3.6 0.7 %copy-start.3 = (bf16[24,256]{1,0:T(8,128)(2,1)S(1)}, bf16[24,256]{1,0:T(8,128)(2,1)}, u32[]{:S(2)}) copy-start(bf16[24,256]{1,0:T(8,128)(2,1)} %zonal.1) | copy-start | bytes 36868
  4.3 0.7 %copy-start.4 = (f32[24,128]{1,0:T(8,128)S(1)}, f32[24,128]{1,0:T(8,128)}, u32[]{:S(2)}) copy-start(f32[24,128]{1,0:T(8,128)} %meridional.1) | copy-start | bytes 36868

commit v2 on v1

--- a/solution.py
+++ b/solution.py
@@ -11,10 +11,11 @@
 LATS, LONS = 32, 8
 CHANNELS = 768
 GROUP = 24
+VMEM_BYTES = 60 * 1024 * 1024
 OWN = 3
 ROWS = 64
 COLS = 128
-Z_STEPS = (1, 7, 2, 6, 3, 5, 4, 0)
+Z_STEPS = (4, 3, 5, 2, 6, 1, 7)
 
 
 def dot(a, b, a_dim=1, b_dim=0):
@@ -32,23 +33,43 @@
     y_lo, z, core = lat // 16, (lat // 2) % 8, lat % 2
     x, y = lon // 2, (lon % 2) * 2 + y_lo
 
-    def around(i, carry):
+    def towards(i):
         x_peer, y_peer = (x + i % 4) % 4, (y + (i // 4) % 4) % 4
-        lat_base = (y_peer % 2) * 16 + (core + i // 16) % 2
-        lon_peer = x_peer * 2 + y_peer // 2
+        return (y_peer % 2) * 16 + (core + i // 16) % 2, x_peer * 2 + y_peer // 2
+
+    def other_planes(i, carry):
+        lat_base, lon_peer = towards(i)
         for step in Z_STEPS:
-            lat_peer = lat_base + ((z + step) % 8) * 2
-            if step:
-                visit(lat_peer, lon_peer)
-            else:
-
-                @pl.when(i != 0)
-                def _():
-                    visit(lat_peer, lon_peer)
-
+            visit(lat_base + ((z + step) % 8) * 2, lon_peer)
         return carry
 
-    lax.fori_loop(0, 32, around, 0)
+    def own_plane(i, carry):
+        lat_base, lon_peer = towards(i)
+        visit(lat_base + z * 2, lon_peer)
+        return carry
+
+    lax.fori_loop(0, 32, other_planes, 0)
+    lax.fori_loop(1, 32, own_plane, 0)
+
+
+def neighbours(lat, lon):
+    y_lo, z, core = lat // 16, (lat // 2) % 8, lat % 2
+    x, y = lon // 2, (lon % 2) * 2 + y_lo
+    column = [
+        (y_lo * 16 + ((z + step) % 8) * 2 + (core + other) % 2, lon)
+        for other in (1, 0)
+        for step in Z_STEPS + (0,)
+        if step or other
+    ]
+    plane = []
+    for y_step in (1, 3, 2, 0):
+        for x_step in (1, 3, 2, 0):
+            if x_step or y_step:
+                x_peer, y_peer = (x + x_step) % 4, (y + y_step) % 4
+                plane.append(
+                    ((y_peer % 2) * 16 + z * 2 + core, x_peer * 2 + y_peer // 2)
+                )
+    return column, plane
 
 
 def reversal(size):
@@ -68,15 +89,24 @@
 
 
 def mixer(
+    signal_hbm,
+    gate_hbm,
+    cotangent_hbm,
+    zonal_hbm,
+    meridional_hbm,
+    mixed_out,
+    gate_out,
+    grad_out,
+    zonal_out,
+    meridional_out,
     signal,
     gate,
     cotangent,
     zonal,
     meridional,
-    conv_out,
-    grad_out,
-    zonal_out,
-    meridional_out,
+    conv_in,
+    mixed,
+    gate_grad,
     zonal_rows,
     grad_src,
     signal_in,
@@ -90,23 +120,43 @@
     taps_in,
     send,
     recv,
+    load,
+    ready,
 ):
     lat, lon = place()
     mine = lat * GROUP + lon * OWN
+    column, plane = neighbours(lat, lon)
     barrier = pltpu.get_barrier_semaphore()
-
-    def greet(lat_peer, lon_peer):
-        pl.semaphore_signal(
-            barrier, inc=1, device_id=(lat_peer, lon_peer), device_id_type=MESH
-        )
-
-    each_peer(lat, lon, greet)
-
+    for peer in column + plane:
+        pl.semaphore_signal(barrier, inc=1, device_id=peer, device_id_type=MESH)
+
+    loads = [
+        pltpu.make_async_copy(source, target, load.at[k])
+        for k, (source, target) in enumerate(
+            (
+                (gate_hbm, gate),
+                (cotangent_hbm, cotangent),
+                (signal_hbm, signal),
+                (zonal_hbm, zonal),
+                (meridional_hbm, meridional),
+            )
+        )
+    ]
+    for copy in loads:
+        copy.start()
+    loads[0].wait()
+    loads[1].wait()
     flat = (CHANNELS * 2, COLS)
-    product = gate.reshape(*flat)[...].astype(F32) * cotangent.reshape(*flat)[...].astype(F32)
+    gate_flat, cotangent_flat = gate.reshape(*flat), cotangent.reshape(*flat)
+    product = gate_flat[...].astype(F32) * cotangent_flat[...].astype(F32)
     grad_src.reshape(*flat)[...] = product.astype(BF16)
-
-    pl.semaphore_wait(barrier, LATS * LONS - 1)
+    for copy in loads[2:]:
+        copy.wait()
+
+    pl.semaphore_wait(barrier, len(column) + len(plane))
+    for peer in plane:
+        pl.semaphore_signal(ready, inc=1, device_id=peer, device_id_type=MESH)
+    pl.semaphore_wait(ready, len(plane))
 
     def spread(source, landing, k):
         def to(lat_peer, lon_peer):
@@ -134,7 +184,9 @@
             ).start()
 
         each_peer(lat, lon, to)
-        landing[pl.ds(mine, OWN)] = source[lon, :, lat]
+        return pltpu.make_async_copy(
+            source.at[lon, :, lat], landing.at[pl.ds(mine, OWN)], load.at[k]
+        )
 
     others = signal.at[pl.ds(0, CHANNELS - OWN)]
 
@@ -180,7 +232,8 @@
         for b in range(LONS):
             conv_view[b, j] = convolved[:, b * COLS : (b + 1) * COLS]
         flipped.append(dot(flip_rows, wide).astype(BF16))
-    give_back(conv_src, conv_out, 2)
+    own_conv = give_back(conv_src, conv_in, 2)
+    own_conv.start()
     for j in range(OWN):
         stack = jnp.concatenate([signal_view[b, j] for b in range(LONS)], axis=0)
         turned = dot(stack, flip_cols).astype(BF16)
@@ -196,7 +249,8 @@
         result = dot(around_circle(blocks), back[j]).astype(BF16)
         for b in range(LONS):
             result_view[b, j] = result[b * ROWS : (b + 1) * ROWS]
-    give_back(result_src, grad_out, 3)
+    own_grad = give_back(result_src, grad_out, 3)
+    own_grad.start()
 
     scale = 1.0 / 256.0
     for j in range(OWN):
@@ -232,28 +286,68 @@
             zonal_out[b * OWN + j : b * OWN + j + 1, :] = taps_in[b, j : j + 1, :256]
             meridional_out[b * OWN + j : b * OWN + j + 1, :] = taps_in[b, j : j + 1, 256:]
 
+    own_conv.wait()
     wait_for(recv.at[2])
+    convolved = conv_in.reshape(*flat)[...].astype(F32)
+    mixed.reshape(*flat)[...] = (gate_flat[...].astype(F32) * convolved).astype(BF16)
+    gate_grad.reshape(*flat)[...] = (cotangent_flat[...].astype(F32) * convolved).astype(BF16)
+    stores = [
+        pltpu.make_async_copy(mixed, mixed_out, load.at[0]),
+        pltpu.make_async_copy(gate_grad, gate_out, load.at[1]),
+    ]
+    for copy in stores:
+        copy.start()
+    for copy in stores + [own_grad]:
+        copy.wait()
     wait_for(recv.at[3])
     for k in range(4):
         wait_for(send.at[k])
     pltpu.make_async_copy(seven, seven, send.at[4]).wait()
 
 
+def place_results(*refs):
+    made, placed, held, (arrived, left) = refs[:5], refs[5:10], refs[10:15], refs[15:]
+    loads = [
+        pltpu.make_async_copy(made[k], held[k], arrived.at[k]) for k in range(len(made))
+    ]
+    stores = [
+        pltpu.make_async_copy(held[k], placed[k], left.at[k]) for k in range(len(made))
+    ]
+    for copy in loads:
+        copy.start()
+    for load, store in zip(loads, stores):
+        load.wait()
+        store.start()
+    for copy in stores:
+        copy.wait()
+
+
 def on_device(signal, gate, cotangent, zonal, meridional):
     field = (CHANNELS, 2, COLS)
     pencil = (LONS, OWN, LATS, 2, COLS)
     in_vmem = pl.BlockSpec(memory_space=pltpu.VMEM)
-    convolved, signal_grad, zonal_grad, meridional_grad = pl.pallas_call(
+    in_hbm = pl.BlockSpec(memory_space=pltpu.HBM)
+    results = [
+        jax.ShapeDtypeStruct(field, BF16),
+        jax.ShapeDtypeStruct(field, BF16),
+        jax.ShapeDtypeStruct(field, BF16),
+        jax.ShapeDtypeStruct((GROUP, 256), F32),
+        jax.ShapeDtypeStruct((GROUP, 128), F32),
+    ]
+    made = pl.pallas_call(
         mixer,
-        out_shape=[
-            jax.ShapeDtypeStruct(field, BF16),
-            jax.ShapeDtypeStruct(field, BF16),
-            jax.ShapeDtypeStruct((GROUP, 256), F32),
-            jax.ShapeDtypeStruct((GROUP, 128), F32),
-        ],
-        in_specs=[in_vmem] * 5,
-        out_specs=[in_vmem] * 4,
+        out_shape=results,
+        in_specs=[in_hbm] * 5,
+        out_specs=[in_hbm] * 3 + [in_vmem] * 2,
         scratch_shapes=[
+            pltpu.VMEM(field, BF16),
+            pltpu.VMEM(field, BF16),
+            pltpu.VMEM(field, BF16),
+            pltpu.VMEM((GROUP, 256), BF16),
+            pltpu.VMEM((GROUP, 128), F32),
+            pltpu.VMEM(field, BF16),
+            pltpu.VMEM(field, BF16),
+            pltpu.VMEM(field, BF16),
             pltpu.VMEM((GROUP, 256), F32),
             pltpu.VMEM(field, BF16),
             pltpu.VMEM(pencil, BF16),
@@ -267,16 +361,24 @@
             pltpu.VMEM((LONS, 8, 384), F32),
             pltpu.SemaphoreType.DMA((5,)),
             pltpu.SemaphoreType.DMA((5,)),
+            pltpu.SemaphoreType.DMA((5,)),
+            pltpu.SemaphoreType.REGULAR,
         ],
         compiler_params=pltpu.CompilerParams(
-            collective_id=0, has_side_effects=True, vmem_limit_bytes=32 * 1024 * 1024
+            collective_id=0, has_side_effects=True, vmem_limit_bytes=VMEM_BYTES
         ),
         name="mixer",
     )(signal, gate, cotangent, zonal, meridional)
-    wide = convolved.astype(F32)
-    mixed = (gate.astype(F32) * wide).astype(BF16)
-    gate_grad = (cotangent.astype(F32) * wide).astype(BF16)
-    return mixed, gate_grad, signal_grad, zonal_grad, meridional_grad
+    return pl.pallas_call(
+        place_results,
+        out_shape=results,
+        in_specs=[in_hbm] * 5,
+        out_specs=[in_hbm] * 5,
+        scratch_shapes=[pltpu.VMEM(shape.shape, shape.dtype) for shape in results]
+        + [pltpu.SemaphoreType.DMA((5,)), pltpu.SemaphoreType.DMA((5,))],
+        compiler_params=pltpu.CompilerParams(vmem_limit_bytes=VMEM_BYTES),
+        name="place_results",
+    )(*made)
 
 
 def solution(mesh):

time: 62.9 us -> 56 us (0.89)
  local copies, waits for them, and re-layouts: 6.34 us -> 0 us
  other arithmetic: 1.59 us -> 0 us
  Pallas kernels: 54 us -> 55.2 us
    unnamed x13 -> x0, local copies, waits for them, and re-layouts: 6.34 us -> none
    convert_element_type x1 -> x0, other arithmetic: 1.59 us -> none  [on_device(): gate_grad = (cotangent.astype(F32) * wide).astype(BF16)]
    pallas_call x1 -> x2, Pallas kernels: 54 us -> 55.2 us  [the longest x1 53.1 us: on_device(): pl.pallas_call(mixer, out_shape=results, in_specs=[in_hbm] * 5, out_specs...]
where the time goes in v2:
time: 56 us; the launch traced here: 55.9 us
  Pallas kernels  55.2 us (99%)
  between operations  0.64 us (1%)
    pallas_call x1, Pallas kernels, on_device(): pl.pallas_call(mixer, out_shape=results, in_specs=[in_hbm] * 5, out_specs...  53.1 us
    pallas_call x1, Pallas kernels, on_device(): pl.pallas_call(place_results, out_shape=results, in_specs=[in_hbm] * 5, o...  2.09 us

profile of v2, /device:TPU:1, one launch (start us, length us, event | category | flops | bytes accessed | tf_op | source)
XLA Modules:
  0.0 55.9 jit_solution(860309573342886640)
XLA Ops:
  0.6 53.1 %mixer.1 = (bf16[768,2,128]{2,1,0:T(2,128)(2,1)}, bf16[768,2,128]{2,1,0:T(2,128)(2,1)}, bf16[768,2,128]{2,1,0:T(2,128)(2,1)}, f32[24,256]{1,0:T(8,128)}, f32[24,128]{1,0:T(8,128)}) custom-call(bf16[768,2,128]{2,1,0:T(2,128)(2,1)} %signal_hbm.1, bf16[768,2,128]{2,1,0:T(2,128)(2,1)} %gate_hbm.1, bf16[768,2,128]{2,1,0:T(2,128)(2,1)} %cotangent_hbm.1, ...), custom_call_target="tpu_custom_call" | custom-call | tf_op jit(solution)/shard_map/mixer/pallas_call | solution.py:337
  53.8 2.1 %place_results.1 = (bf16[768,2,128]{2,1,0:T(2,128)(2,1)}, bf16[768,2,128]{2,1,0:T(2,128)(2,1)}, bf16[768,2,128]{2,1,0:T(2,128)(2,1)}, f32[24,256]{1,0:T(8,128)}, f32[24,128]{1,0:T(8,128)}) custom-call(bf16[768,2,128]{2,1,0:T(2,128)(2,1)} %get-tuple-element.10.refs_0_, bf16[768,2,128]{2,1,0:T(2,128)(2,1)} %get-tuple-element.11.refs_1_, ...), custom_call_target="tpu_custom_call" | custom-call | tf_op jit(solution)/shard_map/place_results/pallas_call | solution.py:372

commit v3 on v2

--- a/solution.py
+++ b/solution.py
@@ -11,7 +11,7 @@
 LATS, LONS = 32, 8
 CHANNELS = 768
 GROUP = 24
-VMEM_BYTES = 60 * 1024 * 1024
+VMEM_BYTES = 32 * 1024 * 1024
 OWN = 3
 ROWS = 64
 COLS = 128
@@ -29,27 +29,32 @@
     return lat, lon
 
 
-def each_peer(lat, lon, visit):
+def each_peer(lat, lon, visit, first=True, rest=True):
+    if first:
+        column, plane = neighbours(lat, lon)
+        for peer in column + plane:
+            visit(*peer)
+    if not rest:
+        return
     y_lo, z, core = lat // 16, (lat // 2) % 8, lat % 2
     x, y = lon // 2, (lon % 2) * 2 + y_lo
 
-    def towards(i):
-        x_peer, y_peer = (x + i % 4) % 4, (y + (i // 4) % 4) % 4
-        return (y_peer % 2) * 16 + (core + i // 16) % 2, x_peer * 2 + y_peer // 2
-
-    def other_planes(i, carry):
-        lat_base, lon_peer = towards(i)
-        for step in Z_STEPS:
-            visit(lat_base + ((z + step) % 8) * 2, lon_peer)
-        return carry
-
-    def own_plane(i, carry):
-        lat_base, lon_peer = towards(i)
-        visit(lat_base + z * 2, lon_peer)
-        return carry
-
-    lax.fori_loop(0, 32, other_planes, 0)
-    lax.fori_loop(1, 32, own_plane, 0)
+    def toward(i, steps, same_core):
+        x_peer, y_peer = (x + i % 4) % 4, (y + i // 4) % 4
+        core_peer = core if same_core else 1 - core
+        lat_base = (y_peer % 2) * 16 + core_peer
+        for step in steps:
+            visit(lat_base + ((z + step) % 8) * 2, x_peer * 2 + y_peer // 2)
+
+    for steps in ((4,), (3, 5), (2, 6), (1, 7), (0,)):
+
+        def around(i, carry):
+            if steps != (0,):
+                toward(i, steps, True)
+            toward(i, steps, False)
+            return carry
+
+        lax.fori_loop(1, 16, around, 0)
 
 
 def neighbours(lat, lon):
@@ -89,7 +94,7 @@
 
 
 def mixer(
-    signal_hbm,
+    signal,
     gate_hbm,
     cotangent_hbm,
     zonal_hbm,
@@ -99,14 +104,11 @@
     grad_out,
     zonal_out,
     meridional_out,
-    signal,
     gate,
     cotangent,
     zonal,
     meridional,
     conv_in,
-    mixed,
-    gate_grad,
     zonal_rows,
     grad_src,
     signal_in,
@@ -136,7 +138,7 @@
             (
                 (gate_hbm, gate),
                 (cotangent_hbm, cotangent),
-                (signal_hbm, signal),
+                (signal.at[pl.ds(mine, OWN)], signal_in.at[lon, :, lat]),
                 (zonal_hbm, zonal),
                 (meridional_hbm, meridional),
             )
@@ -144,21 +146,12 @@
     ]
     for copy in loads:
         copy.start()
-    loads[0].wait()
-    loads[1].wait()
-    flat = (CHANNELS * 2, COLS)
-    gate_flat, cotangent_flat = gate.reshape(*flat), cotangent.reshape(*flat)
-    product = gate_flat[...].astype(F32) * cotangent_flat[...].astype(F32)
-    grad_src.reshape(*flat)[...] = product.astype(BF16)
-    for copy in loads[2:]:
-        copy.wait()
 
     pl.semaphore_wait(barrier, len(column) + len(plane))
     for peer in plane:
         pl.semaphore_signal(ready, inc=1, device_id=peer, device_id_type=MESH)
-    pl.semaphore_wait(ready, len(plane))
-
-    def spread(source, landing, k):
+
+    def spread(source, landing, k, **which):
         def to(lat_peer, lon_peer):
             pltpu.make_async_remote_copy(
                 source.at[pl.ds(lat_peer * GROUP + lon_peer * OWN, OWN)],
@@ -169,8 +162,21 @@
                 device_id_type=MESH,
             ).start()
 
-        each_peer(lat, lon, to)
-        landing[lon, :, lat] = source[pl.ds(mine, OWN)]
+        each_peer(lat, lon, to, **which)
+
+    spread(signal, signal_in, 0, rest=False)
+    for copy in loads:
+        copy.wait()
+    flat = (CHANNELS * 2, COLS)
+    gate_flat, cotangent_flat = gate.reshape(*flat), cotangent.reshape(*flat)
+    product = gate_flat[...].astype(F32) * cotangent_flat[...].astype(F32)
+    grad_src.reshape(*flat)[...] = product.astype(BF16)
+    spread(grad_src, grad_in, 1, rest=False)
+    grad_in[lon, :, lat] = grad_src[pl.ds(mine, OWN)]
+
+    pl.semaphore_wait(ready, len(plane))
+    spread(signal, signal_in, 0, first=False)
+    spread(grad_src, grad_in, 1, first=False)
 
     def give_back(source, landing, k):
         def to(lat_peer, lon_peer):
@@ -188,13 +194,10 @@
             source.at[lon, :, lat], landing.at[pl.ds(mine, OWN)], load.at[k]
         )
 
-    others = signal.at[pl.ds(0, CHANNELS - OWN)]
+    others = gate.at[pl.ds(0, CHANNELS - OWN)]
 
     def wait_for(semaphore):
         pltpu.make_async_copy(others, others, semaphore).wait()
-
-    spread(signal, signal_in, 0)
-    spread(grad_src, grad_in, 1)
 
     zonal_rows[...] = zonal[...].astype(F32)
     for j in range(OWN):
@@ -289,16 +292,9 @@
     own_conv.wait()
     wait_for(recv.at[2])
     convolved = conv_in.reshape(*flat)[...].astype(F32)
-    mixed.reshape(*flat)[...] = (gate_flat[...].astype(F32) * convolved).astype(BF16)
-    gate_grad.reshape(*flat)[...] = (cotangent_flat[...].astype(F32) * convolved).astype(BF16)
-    stores = [
-        pltpu.make_async_copy(mixed, mixed_out, load.at[0]),
-        pltpu.make_async_copy(gate_grad, gate_out, load.at[1]),
-    ]
-    for copy in stores:
-        copy.start()
-    for copy in stores + [own_grad]:
-        copy.wait()
+    mixed_out.reshape(*flat)[...] = (gate_flat[...].astype(F32) * convolved).astype(BF16)
+    gate_out.reshape(*flat)[...] = (cotangent_flat[...].astype(F32) * convolved).astype(BF16)
+    own_grad.wait()
     wait_for(recv.at[3])
     for k in range(4):
         wait_for(send.at[k])
@@ -306,19 +302,14 @@
 
 
 def place_results(*refs):
-    made, placed, held, (arrived, left) = refs[:5], refs[5:10], refs[10:15], refs[15:]
-    loads = [
-        pltpu.make_async_copy(made[k], held[k], arrived.at[k]) for k in range(len(made))
-    ]
-    stores = [
-        pltpu.make_async_copy(held[k], placed[k], left.at[k]) for k in range(len(made))
-    ]
-    for copy in loads:
+    count = len(refs) // 2
+    copies = [
+        pltpu.make_async_copy(refs[k], refs[count + k], refs[-1].at[k])
+        for k in range(count)
+    ]
+    for copy in copies:
         copy.start()
-    for load, store in zip(loads, stores):
-        load.wait()
-        store.start()
-    for copy in stores:
+    for copy in copies:
         copy.wait()
 
 
@@ -328,25 +319,26 @@
     in_vmem = pl.BlockSpec(memory_space=pltpu.VMEM)
     in_hbm = pl.BlockSpec(memory_space=pltpu.HBM)
     results = [
-        jax.ShapeDtypeStruct(field, BF16),
-        jax.ShapeDtypeStruct(field, BF16),
-        jax.ShapeDtypeStruct(field, BF16),
-        jax.ShapeDtypeStruct((GROUP, 256), F32),
-        jax.ShapeDtypeStruct((GROUP, 128), F32),
+        (field, BF16),
+        (field, BF16),
+        (field, BF16),
+        ((GROUP, 256), F32),
+        ((GROUP, 128), F32),
+    ]
+    inputs = [
+        pltpu.with_memory_space_constraint(array, pltpu.HBM)
+        for array in (signal, gate, cotangent, zonal, meridional)
     ]
     made = pl.pallas_call(
         mixer,
-        out_shape=results,
+        out_shape=[pltpu.VMEM(*result) for result in results],
         in_specs=[in_hbm] * 5,
-        out_specs=[in_hbm] * 3 + [in_vmem] * 2,
+        out_specs=[in_vmem] * 5,
         scratch_shapes=[
-            pltpu.VMEM(field, BF16),
             pltpu.VMEM(field, BF16),
             pltpu.VMEM(field, BF16),
             pltpu.VMEM((GROUP, 256), BF16),
             pltpu.VMEM((GROUP, 128), F32),
-            pltpu.VMEM(field, BF16),
-            pltpu.VMEM(field, BF16),
             pltpu.VMEM(field, BF16),
             pltpu.VMEM((GROUP, 256), F32),
             pltpu.VMEM(field, BF16),
@@ -368,17 +360,16 @@
             collective_id=0, has_side_effects=True, vmem_limit_bytes=VMEM_BYTES
         ),
         name="mixer",
-    )(signal, gate, cotangent, zonal, meridional)
+    )(*inputs)
     return pl.pallas_call(
         place_results,
-        out_shape=results,
-        in_specs=[in_hbm] * 5,
+        out_shape=[pltpu.HBM(*result) for result in results],
+        in_specs=[in_vmem] * 5,
         out_specs=[in_hbm] * 5,
-        scratch_shapes=[pltpu.VMEM(shape.shape, shape.dtype) for shape in results]
-        + [pltpu.SemaphoreType.DMA((5,)), pltpu.SemaphoreType.DMA((5,))],
+        scratch_shapes=[pltpu.SemaphoreType.DMA((5,))],
         compiler_params=pltpu.CompilerParams(vmem_limit_bytes=VMEM_BYTES),
         name="place_results",
-    )(*made)
+    )(*[pltpu.with_memory_space_constraint(array, pltpu.VMEM) for array in made])
 
 
 def solution(mesh):

time: 56 us -> 53.6 us (0.957)
  Pallas kernels: 55.2 us -> 52.8 us
    pallas_call x2, Pallas kernels: 55.2 us -> 52.8 us  [the longest x1 51.8 us: on_device(): pl.pallas_call(mixer, out_shape=[pltpu.VMEM(*result) for result in result...]
where the time goes in v3:
time: 53.6 us; the launch traced here: 53.5 us
  Pallas kernels  52.8 us (99%)
  between operations  0.64 us (1%)
    pallas_call x1, Pallas kernels, on_device(): pl.pallas_call(mixer, out_shape=[pltpu.VMEM(*result) for result in result...  51.8 us

profile of v3, /device:TPU:1, one launch (start us, length us, event | category | flops | bytes accessed | tf_op | source)
XLA Modules:
  0.0 53.5 jit_solution(6068684691396545918)
XLA Ops:
  0.6 51.8 %mixer.1 = (bf16[768,2,128]{2,1,0:T(2,128)(2,1)S(1)}, bf16[768,2,128]{2,1,0:T(2,128)(2,1)S(1)}, bf16[768,2,128]{2,1,0:T(2,128)(2,1)S(1)}, f32[24,256]{1,0:T(8,128)S(1)}, f32[24,128]{1,0:T(8,128)S(1)}) custom-call(bf16[768,2,128]{2,1,0:T(2,128)(2,1)} %signal.1, bf16[768,2,128]{2,1,0:T(2,128)(2,1)} %gate_hbm.1, bf16[768,2,128]{2,1,0:T(2,128)(2,1)} %cotangent_hbm.1, ...), custom_call_target="tpu_custom_call" | custom-call | tf_op jit(solution)/shard_map/mixer/pallas_call | solution.py:332
  52.4 1.1 %place_results.1 = (bf16[768,2,128]{2,1,0:T(2,128)(2,1)}, bf16[768,2,128]{2,1,0:T(2,128)(2,1)}, bf16[768,2,128]{2,1,0:T(2,128)(2,1)}, f32[24,256]{1,0:T(8,128)}, f32[24,128]{1,0:T(8,128)}) custom-call(bf16[768,2,128]{2,1,0:T(2,128)(2,1)S(1)} %get-tuple-element.10.refs_0_, bf16[768,2,128]{2,1,0:T(2,128)(2,1)S(1)} %get-tuple-element.11.refs_1_, ...), custom_call_target="tpu_custom_call" | custom-call | tf_op jit(solution)/shard_map/place_results/pallas_call | solution.py:364

commit v4 on v3

--- a/solution.py
+++ b/solution.py
@@ -46,10 +46,10 @@
         for step in steps:
             visit(lat_base + ((z + step) % 8) * 2, x_peer * 2 + y_peer // 2)
 
-    for steps in ((4,), (3, 5), (2, 6), (1, 7), (0,)):
+    for steps in (Z_STEPS, (0,)):
 
         def around(i, carry):
-            if steps != (0,):
+            if steps is Z_STEPS:
                 toward(i, steps, True)
             toward(i, steps, False)
             return carry
@@ -176,9 +176,8 @@
 
     pl.semaphore_wait(ready, len(plane))
     spread(signal, signal_in, 0, first=False)
-    spread(grad_src, grad_in, 1, first=False)
-
-    def give_back(source, landing, k):
+
+    def give_back(source, landing, k, corner_first=False):
         def to(lat_peer, lon_peer):
             pltpu.make_async_remote_copy(
                 source.at[lon_peer, :, lat_peer],
@@ -189,7 +188,19 @@
                 device_id_type=MESH,
             ).start()
 
-        each_peer(lat, lon, to)
+        if corner_first:
+            for corner in range(2):
+
+                @pl.when((lat != corner) | (lon != 0))
+                def _():
+                    to(corner, 0)
+
+        def unless_corner(lat_peer, lon_peer):
+            @pl.when((lat_peer > 1) | (lon_peer > 0))
+            def _():
+                to(lat_peer, lon_peer)
+
+        each_peer(lat, lon, unless_corner if corner_first else to)
         return pltpu.make_async_copy(
             source.at[lon, :, lat], landing.at[pl.ds(mine, OWN)], load.at[k]
         )
@@ -218,6 +229,8 @@
         lat_weights[j] = turned.astype(BF16)
     flip_cols, flip_rows = reversal(COLS), reversal(ROWS)
 
+    spread(grad_src, grad_in, 1, first=False)
+
     signal_view = signal_in.reshape(LONS, OWN, ROWS, COLS)
     grad_view = grad_in.reshape(LONS, OWN, ROWS, COLS)
     conv_view = conv_src.reshape(LONS, OWN, ROWS, COLS)
@@ -252,7 +265,7 @@
         result = dot(around_circle(blocks), back[j]).astype(BF16)
         for b in range(LONS):
             result_view[b, j] = result[b * ROWS : (b + 1) * ROWS]
-    own_grad = give_back(result_src, grad_out, 3)
+    own_grad = give_back(result_src, grad_out, 3, corner_first=True)
     own_grad.start()
 
     scale = 1.0 / 256.0

time: 53.6 us -> 51.3 us (0.957)
  the two profiles are of different devices: /device:TPU:1 before, /device:TPU:32 now
where the time goes in v4:
time: 51.3 us; the launch traced here: 50.6 us
  Pallas kernels  49.9 us (97%)
  between operations  0.64 us (1%)
    pallas_call x1, Pallas kernels, on_device(): pl.pallas_call(mixer, out_shape=[pltpu.VMEM(*result) for result in result...  48.9 us
    pallas_call x1, Pallas kernels, on_device(): pl.pallas_call(place_results, out_shape=[pltpu.HBM(*result) for result in...  1.06 us

profile of v4, /device:TPU:32, one launch (start us, length us, event | category | flops | bytes accessed | tf_op | source)
XLA Modules:
  0.0 50.6 jit_solution(11113668335513204866)
XLA Ops:
  0.6 48.9 %mixer.1 = (bf16[768,2,128]{2,1,0:T(2,128)(2,1)S(1)}, bf16[768,2,128]{2,1,0:T(2,128)(2,1)S(1)}, bf16[768,2,128]{2,1,0:T(2,128)(2,1)S(1)}, f32[24,256]{1,0:T(8,128)S(1)}, f32[24,128]{1,0:T(8,128)S(1)}) custom-call(bf16[768,2,128]{2,1,0:T(2,128)(2,1)} %signal.1, bf16[768,2,128]{2,1,0:T(2,128)(2,1)} %gate_hbm.1, bf16[768,2,128]{2,1,0:T(2,128)(2,1)} %cotangent_hbm.1, ...), custom_call_target="tpu_custom_call" | custom-call | tf_op jit(solution)/shard_map/mixer/pallas_call | solution.py:345
  49.5 1.1 %place_results.1 = (bf16[768,2,128]{2,1,0:T(2,128)(2,1)}, bf16[768,2,128]{2,1,0:T(2,128)(2,1)}, bf16[768,2,128]{2,1,0:T(2,128)(2,1)}, f32[24,256]{1,0:T(8,128)}, f32[24,128]{1,0:T(8,128)}) custom-call(bf16[768,2,128]{2,1,0:T(2,128)(2,1)S(1)} %get-tuple-element.10.refs_0_, bf16[768,2,128]{2,1,0:T(2,128)(2,1)S(1)} %get-tuple-element.11.refs_1_, ...), custom_call_target="tpu_custom_call" | custom-call | tf_op jit(solution)/shard_map/place_results/pallas_call | solution.py:377

commit v5 on v4

--- a/solution.py
+++ b/solution.py
@@ -18,6 +18,12 @@
 Z_STEPS = (4, 3, 5, 2, 6, 1, 7)
 
 
+PLANE_STEPS = (
+    (2, 2), (1, 2), (3, 2), (2, 1), (2, 3), (1, 1), (3, 3), (1, 3),
+    (3, 1), (2, 0), (0, 2), (1, 0), (3, 0), (0, 1), (0, 3),
+)
+
+
 def dot(a, b, a_dim=1, b_dim=0):
     return lax.dot_general(
         a, b, (((a_dim,), (b_dim,)), ((), ())), preferred_element_type=F32
@@ -39,8 +45,8 @@
     y_lo, z, core = lat // 16, (lat // 2) % 8, lat % 2
     x, y = lon // 2, (lon % 2) * 2 + y_lo
 
-    def toward(i, steps, same_core):
-        x_peer, y_peer = (x + i % 4) % 4, (y + i // 4) % 4
+    def toward(x_step, y_step, steps, same_core):
+        x_peer, y_peer = (x + x_step) % 4, (y + y_step) % 4
         core_peer = core if same_core else 1 - core
         lat_base = (y_peer % 2) * 16 + core_peer
         for step in steps:
@@ -48,13 +54,19 @@
 
     for steps in (Z_STEPS, (0,)):
 
-        def around(i, carry):
+        def around(i, digits):
+            x_digits, y_digits = digits
+            x_step, y_step = x_digits % 4, y_digits % 4
             if steps is Z_STEPS:
-                toward(i, steps, True)
-            toward(i, steps, False)
-            return carry
-
-        lax.fori_loop(1, 16, around, 0)
+                toward(x_step, y_step, steps, True)
+            toward(x_step, y_step, steps, False)
+            return x_digits // 4, y_digits // 4
+
+        digits = [
+            jnp.int32(sum(step[axis] * 4**i for i, step in enumerate(PLANE_STEPS)))
+            for axis in range(2)
+        ]
+        lax.fori_loop(0, len(PLANE_STEPS), around, tuple(digits))
 
 
 def neighbours(lat, lon):
@@ -200,7 +212,9 @@
             def _():
                 to(lat_peer, lon_peer)
 
-        each_peer(lat, lon, unless_corner if corner_first else to)
+        visit = unless_corner if corner_first else to
+        each_peer(lat, lon, visit, first=False)
+        each_peer(lat, lon, visit, rest=False)
         return pltpu.make_async_copy(
             source.at[lon, :, lat], landing.at[pl.ds(mine, OWN)], load.at[k]
         )

time: 51.3 us -> 50.1 us (0.977)
  Pallas kernels: 49.9 us -> 48.9 us
    pallas_call x1, Pallas kernels: 48.9 us -> 47.8 us  [on_device(): pl.pallas_call(mixer, out_shape=[pltpu.VMEM(*result) for result in result...]
where the time goes in v5:
time: 50.1 us; the launch traced here: 49.5 us
  Pallas kernels  48.9 us (98%)
  between operations  0.64 us (1%)
    pallas_call x1, Pallas kernels, on_device(): pl.pallas_call(mixer, out_shape=[pltpu.VMEM(*result) for result in result...  47.8 us
    pallas_call x1, Pallas kernels, on_device(): pl.pallas_call(place_results, out_shape=[pltpu.HBM(*result) for result in...  1.06 us

profile of v5, /device:TPU:32, one launch (start us, length us, event | category | flops | bytes accessed | tf_op | source)
XLA Modules:
  0.0 49.5 jit_solution(15887950626154774081)
XLA Ops:
  0.6 47.8 %mixer.1 = (bf16[768,2,128]{2,1,0:T(2,128)(2,1)S(1)}, bf16[768,2,128]{2,1,0:T(2,128)(2,1)S(1)}, bf16[768,2,128]{2,1,0:T(2,128)(2,1)S(1)}, f32[24,256]{1,0:T(8,128)S(1)}, f32[24,128]{1,0:T(8,128)S(1)}) custom-call(bf16[768,2,128]{2,1,0:T(2,128)(2,1)} %signal.1, bf16[768,2,128]{2,1,0:T(2,128)(2,1)} %gate_hbm.1, bf16[768,2,128]{2,1,0:T(2,128)(2,1)} %cotangent_hbm.1, ...), custom_call_target="tpu_custom_call" | custom-call | tf_op jit(solution)/shard_map/mixer/pallas_call | solution.py:359
  48.5 1.1 %place_results.1 = (bf16[768,2,128]{2,1,0:T(2,128)(2,1)}, bf16[768,2,128]{2,1,0:T(2,128)(2,1)}, bf16[768,2,128]{2,1,0:T(2,128)(2,1)}, f32[24,256]{1,0:T(8,128)}, f32[24,128]{1,0:T(8,128)}) custom-call(bf16[768,2,128]{2,1,0:T(2,128)(2,1)S(1)} %get-tuple-element.10.refs_0_, bf16[768,2,128]{2,1,0:T(2,128)(2,1)S(1)} %get-tuple-element.11.refs_1_, ...), custom_call_target="tpu_custom_call" | custom-call | tf_op jit(solution)/shard_map/place_results/pallas_call | solution.py:391

commit v6 on v5

--- a/solution.py
+++ b/solution.py
@@ -50,7 +50,7 @@
         core_peer = core if same_core else 1 - core
         lat_base = (y_peer % 2) * 16 + core_peer
         for step in steps:
-            visit(lat_base + ((z + step) % 8) * 2, x_peer * 2 + y_peer // 2)
+            visit(lat_base + ((z + step + core * (8 - 2 * step)) % 8) * 2, x_peer * 2 + y_peer // 2)
 
     for steps in (Z_STEPS, (0,)):
 

time: 50.1 us -> 50.2 us (level)
  no operation moved by 1% of the time
where the time goes in v6:
time: 50.2 us; the launch traced here: 49.5 us
  Pallas kernels  48.9 us (97%)
  between operations  0.64 us (1%)
    pallas_call x1, Pallas kernels, on_device(): pl.pallas_call(mixer, out_shape=[pltpu.VMEM(*result) for result in result...  47.8 us
    pallas_call x1, Pallas kernels, on_device(): pl.pallas_call(place_results, out_shape=[pltpu.HBM(*result) for result in...  1.06 us

profile of v6, /device:TPU:32, one launch (start us, length us, event | category | flops | bytes accessed | tf_op | source)
XLA Modules:
  0.0 49.5 jit_solution(13878915197268274568)
XLA Ops:
  0.6 47.8 %mixer.1 = (bf16[768,2,128]{2,1,0:T(2,128)(2,1)S(1)}, bf16[768,2,128]{2,1,0:T(2,128)(2,1)S(1)}, bf16[768,2,128]{2,1,0:T(2,128)(2,1)S(1)}, f32[24,256]{1,0:T(8,128)S(1)}, f32[24,128]{1,0:T(8,128)S(1)}) custom-call(bf16[768,2,128]{2,1,0:T(2,128)(2,1)} %signal.1, bf16[768,2,128]{2,1,0:T(2,128)(2,1)} %gate_hbm.1, bf16[768,2,128]{2,1,0:T(2,128)(2,1)} %cotangent_hbm.1, ...), custom_call_target="tpu_custom_call" | custom-call | tf_op jit(solution)/shard_map/mixer/pallas_call | solution.py:359
  48.5 1.1 %place_results.1 = (bf16[768,2,128]{2,1,0:T(2,128)(2,1)}, bf16[768,2,128]{2,1,0:T(2,128)(2,1)}, bf16[768,2,128]{2,1,0:T(2,128)(2,1)}, f32[24,256]{1,0:T(8,128)}, f32[24,128]{1,0:T(8,128)}) custom-call(bf16[768,2,128]{2,1,0:T(2,128)(2,1)S(1)} %get-tuple-element.10.refs_0_, bf16[768,2,128]{2,1,0:T(2,128)(2,1)S(1)} %get-tuple-element.11.refs_1_, ...), custom_call_target="tpu_custom_call" | custom-call | tf_op jit(solution)/shard_map/place_results/pallas_call | solution.py:391
